TPU v7x, 512 devices: a whole 4x4x16 slice. The times are simulated.
512 devices in a mesh: row: 32 (over y, x, z_hi), col: 16 (over z_lo, core).
Axes of the slice: x: 4, y: 4, z: 16 (z_hi: 2, z_lo: 8; z = z_hi * 8 + z_lo), core: 2. Of those that a mesh axis runs over, the one named last changes fastest.
Arguments:
- kernel_tiles: float32 [32, 16, 32, 128, 128], P('row', 'col'), may hold values from -0.0234375 to 0.0234375
- basis: float32 [64, 32, 16, 128], P(None, 'row', 'col'), may hold values from -6 to 6
Outputs:
- orthobasis: float32 [64, 32, 16, 128], P(None, 'row', 'col')
- cholesky_factor: float32 [64, 64], replicated
All inputs are finite; a program needn't handle non-finite values.
Results may differ from a plain program's by a relative error of at most 0.0003.
Values sent between devices are 32-bit elements; how exact they have to be, the bound alone decides.
A program may use at most 64 MiB of HBM per device.

v0:
```python
import jax
import jax.numpy as jnp
from jax import lax
from jax.sharding import PartitionSpec as P

ITERS = 2


def per_device(kernel_tiles, basis):
    highest = lax.Precision.HIGHEST
    row_count = lax.axis_size("row")
    col_count = lax.axis_size("col")
    row_id = lax.axis_index("row")
    col_id = lax.axis_index("col")
    kernel_local = kernel_tiles[0, 0]
    ct_total = kernel_local.shape[0]
    tile_size = kernel_local.shape[1]
    sub_count = basis.shape[0]
    local_tiles = ct_total // row_count
    order_total = ct_total * col_count * tile_size
    band_block = row_id // col_count
    band_col = row_id % col_count
    root_flag = (col_id == band_col).astype(jnp.float32)
    diag_tile = lax.dynamic_index_in_dim(kernel_local, band_block, 0, keepdims=False)
    sym_diag = 0.5 * (diag_tile + diag_tile.T)
    factor = basis.reshape(sub_count, local_tiles, tile_size)
    cholesky_factor = jnp.zeros((sub_count, sub_count), jnp.float32)
    for step_index in range(ITERS):
        pieces = lax.all_gather(factor, "row", axis=1, tiled=True)
        piece_count = pieces.shape[1]
        block_ids = jnp.arange(piece_count, dtype=jnp.int32)
        upper_mask = (block_ids * col_count + col_id > row_id).astype(jnp.float32)
        direct = jnp.einsum(
            "bts,kbs->kt", kernel_local, pieces * upper_mask[None, :, None], precision=highest
        )
        pick_mask = (block_ids == band_block).astype(jnp.float32) * root_flag
        own_tile = jnp.einsum("kbt,b->kt", pieces, pick_mask, precision=highest)
        direct, own_tile = (direct, own_tile)
        direct = direct + root_flag * jnp.dot(own_tile, sym_diag.T, precision=highest)
        total_direct, band_vector = lax.psum((direct, own_tile), "col")
        transposed_block_ids = jnp.arange(lax.axis_size("row") * local_tiles, dtype=jnp.int32)
        transposed_upper_mask = (transposed_block_ids * col_count + col_id > row_id).astype(
            jnp.float32
        )
        tile_terms = (
            jnp.einsum("bts,kt->bks", kernel_local, band_vector, precision=highest)
            * transposed_upper_mask[:, None, None]
        )
        shares = lax.psum_scatter(tile_terms, "row", scatter_dimension=0, tiled=True)
        product = jnp.transpose(shares, (1, 0, 2))
        every_row = lax.all_gather(total_direct[:, None, :], "row", axis=1, tiled=True)
        held_ids = (
            row_id * local_tiles + jnp.arange(local_tiles, dtype=jnp.int32)
        ) * col_count + col_id
        select_map = (jnp.arange(row_count, dtype=jnp.int32)[:, None] == held_ids[None, :]).astype(
            jnp.float32
        )
        product = product + jnp.einsum("krt,rb->kbt", every_row, select_map, precision=highest)
        gram_part = jnp.einsum("kbt,lbt->kl", product, product, precision=highest)
        gram_sum = lax.psum(gram_part, ("row", "col")) / order_total
        cholesky_factor = jnp.linalg.cholesky(gram_sum)
        solved = jax.scipy.linalg.solve_triangular(
            cholesky_factor, product.reshape(sub_count, local_tiles * tile_size), lower=True
        )
        factor = solved.reshape(sub_count, local_tiles, tile_size)
    return (factor.reshape(sub_count, local_tiles, 1, tile_size), cholesky_factor)


def solution(mesh):
    placed = (P("row", "col", None, None, None), P(None, "row", "col", None))
    return jax.shard_map(
        per_device,
        mesh=mesh,
        in_specs=placed,
        out_specs=(P(None, "row", "col", None), P()),
        check_vma=False,
    )
```

profile of v0, /device:TPU:1, one launch (start us, length us, event | category | flops | bytes accessed | tf_op | source)
XLA Modules:
  0.0 1675.4 jit_solution(6278756103466736351)
XLA Ops:
  7.2 0.7 all-gather.11.cloned.1.call-update
  8.0 0.8 copy-done
  8.9 119.0 %all-gather.11.cloned.1.call-done = f32[64,32,1,128]{3,0,2,1:T(8,128)} async-done(((f32[64,1,1,128]{3,0,2,1:T(8,128)}), f32[64,32,1,128]{3,0,2,1:T(8,128)}) %all-gather.11.cloned.1.call-update) | async-done | bytes 1048592 | tf_op jit(solution)/shard_map/all_gather | solution.py:29
  127.9 2.4 fusion.35
  130.3 3.5 fusion.20
  133.8 0.9 fusion.29
  134.7 174.3 %all-reduce.7.cloned.1.call-done = (f32[64,1,128]{2,0,1:T(8,128)}, f32[64,128]{1,0:T(8,128)}) async-done(((f32[64,1,128]{2,0,1:T(8,128)}, f32[64,128]{1,0:T(8,128)}), (f32[64,1,128]{2,0,1:T(8,128)}, f32[64,128]{1,0:T(8,128)})) %all-reduce.7.cloned.1.call-update) | async-done | bytes 65552 | tf_op jit(solution)/shard_map/psum | solution.py:40
  309.1 3.0 fusion.11
  312.2 114.4 %all-gather.7.cloned.1.call-done = f32[64,32,128]{2,0,1:T(8,128)} async-done(((f32[64,1,128]{2,0,1:T(8,128)}), f32[64,32,128]{2,0,1:T(8,128)}) %all-gather.7.cloned.1.call-update) | async-done | bytes 1048592 | tf_op jit(solution)/shard_map/all_gather | solution.py:51
  426.5 2.2 fusion.33
  428.8 277.6 %reduce-scatter.3.cloned.1.call-done = f32[1,64,128]{2,1,0:T(8,128)} async-done(((f32[32,64,128]{2,1,0:T(8,128)}), f32[1,64,128]{2,1,0:T(8,128)}) %reduce-scatter.3.cloned.1.call-update) | async-done | bytes 32784 | tf_op jit(solution)/shard_map/reduce_scatter | solution.py:49
  706.4 1.0 fusion.55
  707.4 123.2 %psum.44 = f32[64,64]{0,1:T(8,128)S(1)} all-reduce(f32[64,64]{0,1:T(8,128)S(1)} %fusion.55), channel_id=1, replica_groups=mesh['row'=32,'col'=16] {'row','col'}, use_global_device_ids=true, to_apply=%region_3.4 | all-reduce | flops 4096 | bytes 32768 | tf_op jit(solution)/shard_map/psum | solution.py:60
  830.7 5.8 cholesky.44
  837.9 4.9 custom-call.6
  842.8 1.6 fusion.46
  844.5 108.4 %all-gather.13.cloned.1.call-done = f32[64,4096]{1,0:T(8,128)} async-done(((f32[64,128]{1,0:T(8,128)}), f32[64,4096]{1,0:T(8,128)}) %all-gather.13.cloned.1.call-update) | async-done | bytes 1048592 | tf_op jit(solution)/shard_map/all_gather | solution.py:29
  952.9 1.5 copy.37
  954.4 0.7 fusion.66
  955.1 2.3 fusion.23
  957.5 0.9 fusion.27
  958.4 174.3 %all-reduce.5.cloned.1.call-done = (f32[64,1,128]{2,0,1:T(8,128)}, f32[64,128]{1,0:T(8,128)}) async-done(((f32[64,1,128]{2,0,1:T(8,128)}, f32[64,128]{1,0:T(8,128)}), (f32[64,1,128]{2,0,1:T(8,128)}, f32[64,128]{1,0:T(8,128)})) %all-reduce.5.cloned.1.call-update) | async-done | bytes 65552 | tf_op jit(solution)/shard_map/psum | solution.py:40
  1132.9 3.0 fusion.17
  1135.9 114.3 %all-gather.9.cloned.1.call-done = f32[64,32,128]{2,0,1:T(8,128)} async-done(((f32[64,1,128]{2,0,1:T(8,128)}), f32[64,32,128]{2,0,1:T(8,128)}) %all-gather.9.cloned.1.call-update) | async-done | bytes 1048592 | tf_op jit(solution)/shard_map/all_gather | solution.py:51
  1250.2 2.2 fusion.31
  1252.4 277.7 %reduce-scatter.5.cloned.1.call-done = f32[1,64,128]{2,1,0:T(8,128)} async-done(((f32[32,64,128]{2,1,0:T(8,128)}), f32[1,64,128]{2,1,0:T(8,128)}) %reduce-scatter.5.cloned.1.call-update) | async-done | bytes 32784 | tf_op jit(solution)/shard_map/reduce_scatter | solution.py:49
  1530.1 1.0 fusion.56
  1531.2 123.0 %psum.47 = f32[64,64]{0,1:T(8,128)S(1)} all-reduce(f32[64,64]{0,1:T(8,128)S(1)} %fusion.56), channel_id=1, replica_groups=mesh['row'=32,'col'=16] {'row','col'}, use_global_device_ids=true, to_apply=%region_9.12 | all-reduce | flops 4096 | bytes 32768 | tf_op jit(solution)/shard_map/psum | solution.py:60
  1654.3 5.8 cholesky.55
  1660.8 1.3 select_bitcast_fusion
  1662.1 4.9 custom-call.7
  1667.0 1.6 fusion.42
  (36 shorter events, 2.9 us)
Async XLA Ops:
  7.2 1.6 copy-start
  7.2 120.7 %all-gather.11.cloned.1.call-start = ((), (), s32[]{:S(2)}) async-start(), calls=%async_computation.6 | async-start | bytes 1081344 | tf_op jit(solution)/shard_map/all_gather | solution.py:29
  7.9 301.1 %all-reduce.7.cloned.1.call-start = ((), (), s32[]{:S(2)}) async-start(), calls=%async_computation.9 | async-start | bytes 131072 | tf_op jit(solution)/shard_map/psum | solution.py:40
  130.2 4.4 copy-start.3
  134.7 291.9 %all-gather.7.cloned.1.call-start = ((), (), s32[]{:S(2)}) async-start(), calls=%async_computation.3 | async-start | bytes 1081344 | tf_op jit(solution)/shard_map/all_gather | solution.py:51
  309.0 397.4 %reduce-scatter.3.cloned.1.call-start = ((), (), s32[]{:S(2)}) async-start(), calls=%async_computation.2 | async-start | bytes 1081344 | tf_op jit(solution)/shard_map/reduce_scatter | solution.py:49
  312.1 640.8 %all-gather.13.cloned.1.call-start = ((), (), s32[]{:S(2)}) async-start(), calls=%async_computation.7 | async-start | bytes 1081344 | tf_op jit(solution)/shard_map/all_gather | solution.py:29
  844.5 288.2 %all-reduce.5.cloned.1.call-start = ((), (), s32[]{:S(2)}) async-start(), calls=%async_computation.8 | async-start | bytes 131072 | tf_op jit(solution)/shard_map/psum | solution.py:40
  952.9 2.2 copy-start.1
  955.1 3.2 copy-start.2
  958.3 291.9 %all-gather.9.cloned.1.call-start = ((), (), s32[]{:S(2)}) async-start(), calls=%async_computation.5 | async-start | bytes 1081344 | tf_op jit(solution)/shard_map/all_gather | solution.py:51
  1132.7 397.4 %reduce-scatter.5.cloned.1.call-start = ((), (), s32[]{:S(2)}) async-start(), calls=%async_computation.4 | async-start | bytes 1081344 | tf_op jit(solution)/shard_map/reduce_scatter | solution.py:49
Sparse Core Ops, SparseCore 0:
  12.3 115.5 all-gather.10
  134.8 174.1 all-reduce.6
  314.1 112.4 all-gather.6
  429.4 276.9 reduce-scatter.2
  844.6 108.3 all-gather.12
  958.5 174.1 all-reduce.4
  1137.7 112.4 all-gather.8
  1253.2 276.8 reduce-scatter.4
where the time goes:
time: 1680 us
  waiting for transfers between devices  1360 us (81%)
  blocking collectives  246 us (15%)
  matrix products  26.3 us (2%)
  other arithmetic  24.8 us (1%)
    reduce_scatter x2, waiting for transfers between devices, per_device(): lax.psum_scatter(tile_terms, 'row', scatter_dimension=0, tiled=True)  555 us
    psum x2, waiting for transfers between devices, per_device(): total_direct, band_vector = lax.psum((direct, own_tile), 'col')  349 us
    psum x2, blocking collectives, per_device(): gram_sum = lax.psum(gram_part, ('row', 'col')) / order_total  246 us
    all_gather x2, waiting for transfers between devices, per_device(): lax.all_gather(total_direct[:, None, :], 'row', axis=1, tiled=True)  229 us
    all_gather x2, waiting for transfers between devices, per_device(): pieces = lax.all_gather(factor, 'row', axis=1, tiled=True)  227 us
  transfers between devices with their start and end apart: 8, of which 8 were waited for; matrix products, arithmetic and copies ran while one was open for 1% of the time, Pallas kernels for 0%

commit v1 on v0

v1 whole, which is shorter than its diff:
```python
import functools

import jax
import jax.numpy as jnp
from jax import lax
from jax.experimental import pallas as pl
from jax.experimental.pallas import tpu as pltpu
from jax.sharding import PartitionSpec as P

MESH = pl.DeviceIdType.MESH
HI = lax.Precision.HIGHEST
F32 = jnp.float32
BF16 = jnp.bfloat16


def split(x):
    hi = x.astype(BF16)
    return hi, (x - hi.astype(F32)).astype(BF16)


def nt(a, b):
    return lax.dot_general(a, b, (((1,), (1,)), ((), ())), preferred_element_type=F32)


def nt_high(a, b):
    return lax.dot_general(
        a, b, (((1,), (1,)), ((), ())), precision=HI, preferred_element_type=F32
    )


def factorize(gram):
    n = gram.shape[0]
    eye = (
        lax.broadcasted_iota(jnp.int32, (n, n), 0) == lax.broadcasted_iota(jnp.int32, (n, n), 1)
    ).astype(F32)
    full = jnp.concatenate([gram, eye], axis=1)
    blocks = [full[8 * j : 8 * j + 8] for j in range(n // 8)]
    below = lax.broadcasted_iota(jnp.int32, (8, 1), 0)
    for k in range(n):
        at, sub = divmod(k, 8)
        row = blocks[at][sub : sub + 1]
        pivot = row[:, k : k + 1]
        scaled = row * (1.0 / pivot)
        for j in range(at, n // 8):
            column = blocks[j][:, k : k + 1]
            if j == at:
                column = jnp.where(below > sub, column, 0.0)
            blocks[j] = blocks[j] - column * scaled
    full = jnp.concatenate(blocks, axis=0)
    diagonal = jnp.sum(full[:, :n] * eye, axis=1, keepdims=True)
    return full * lax.rsqrt(diagonal)


def kernel(nrow, ncol, k_ref, v_ref, out_ref, chol_ref, *scratch):
    (
        kh, kl, vc, ktr, vg0, vg1, ps1, ps2, pr1, pr2, zs1, zr1, zs2, zr2, troot,
        ds1, dr1, ds2, dr2, tp0, tg0, tg1, hs, hp, hz,
        gs, gr, gp, gz, gq, ga,
        kq, tps, z_sem, ag_sem, rs_sem, col_sem, top_sem, hz_sem, g_sem,
        s_one, s_xy, s_rs, s_col, s_top, s_g, s_h,
    ) = scratch
    nxy = nrow // 2
    nline = 2 * ncol
    band = nrow // ncol
    row, col = lax.axis_index("row"), lax.axis_index("col")
    xy, zh = row // 2, row % 2
    other = 1 - zh
    sub, tile = v_ref.shape
    order = nrow * ncol * tile
    member = zh * ncol + col
    home = row // ncol
    is_root = col == row % ncol
    holds = row < band
    self_held = jnp.logical_and(row == home, is_root)
    zpart = (xy * 2 + other, col)

    def plane(k):
        return (lax.rem(xy + k, nxy) * 2 + zh, col)

    def in_col(k):
        return (row, lax.rem(col + k, ncol))

    def in_line(k):
        at = lax.rem(member + k, nline)
        return (xy * 2 + at // ncol, lax.rem(at, ncol))

    def mirror(b):
        return (b * ncol + col, lax.rem(row, ncol))

    def holder():
        return (home, lax.rem(row, ncol))

    def held_member(p):
        return (row * ncol + col, p)

    def each(n, body, start=1):
        def step(k, carry):
            body(k)
            return carry

        lax.fori_loop(start, n, step, 0)

    def push(src, dst, s, r, where):
        pltpu.make_async_remote_copy(
            src_ref=src, dst_ref=dst, send_sem=s, recv_sem=r, device_id=where, device_id_type=MESH
        ).start()

    def take(ref, sem):
        pltpu.make_async_copy(ref, ref, sem).wait()

    bar = pltpu.get_barrier_semaphore()

    def greet(where):
        pl.semaphore_signal(bar, inc=1, device_id=where, device_id_type=MESH)

    each(nxy, lambda k: greet(plane(k)))
    each(nline, lambda k: greet(in_line(k)))
    for b in range(band):
        pl.when(b * ncol + col != row)(functools.partial(lambda b: greet(mirror(b)), b))
    pl.when(jnp.logical_not(self_held))(lambda: greet(holder()))

    @pl.when(holds)
    def _():
        def one(p):
            same = jnp.logical_and(row * ncol + col == row, p == col)
            pl.when(jnp.logical_not(same))(lambda: greet(held_member(p)))

        each(ncol, one, 0)

    def cut(q):
        for zd in range(2):
            hi, lo = split(k_ref[2 * q + zd])
            kh[zd, :, q * tile : (q + 1) * tile] = hi
            kl[zd, :, q * tile : (q + 1) * tile] = lo

    for q in range(1, nxy):
        cut(q)
    tile0 = v_ref[...]
    vg0[zh, xy] = tile0

    @pl.when(holds)
    def _():
        spread = jnp.concatenate([tile0, tile0], axis=0).T
        hs[...] = spread.reshape(hs.shape)

    greeted = (nxy - 1) + (nline - 1) + band - is_root.astype(jnp.int32)
    greeted = greeted + jnp.where(self_held, 0, 1)
    greeted = greeted + jnp.where(holds, ncol, 0) - jnp.where(self_held, 1, 0)
    pl.semaphore_wait(bar, greeted)

    push(v_ref, vg0.at[zh, xy], s_one.at[0], z_sem.at[0], zpart)

    @pl.when(holds)
    def _():
        def one(p):
            same = jnp.logical_and(row * ncol + col == row, p == col)
            pl.when(jnp.logical_not(same))(
                lambda: push(hs.at[p], tp0, s_h.at[0], tps.at[0], held_member(p))
            )

        each(ncol, one, 0)

    each(nxy, lambda k: push(v_ref, vg0.at[zh, xy], s_xy.at[0], ag_sem.at[0, 0], plane(k)))
    for b in range(band):

        @pl.when(row < b * ncol + col)
        def _(b=b):
            push(k_ref.at[b], ktr.at[home], s_one.at[4 + b], kq.at[home], mirror(b))

    def all_in_col(src, dst, n):
        each(ncol, lambda k: push(src, dst, s_col.at[n], col_sem.at[n], in_col(k)))

    @pl.when(self_held)
    def _():
        tp0[...] = hs[col]

    @pl.when(jnp.logical_not(self_held))
    def _():
        take(tp0, tps.at[0])

    tg0[col] = tp0[...]
    all_in_col(tp0, tg0.at[col], 0)

    take(vg0.at[other, xy], z_sem.at[0])
    each(
        nxy,
        lambda k: push(
            vg0.at[other, xy], vg0.at[other, xy], s_xy.at[1], ag_sem.at[0, 1], plane(k)
        ),
    )

    def upright(pieces):
        return pieces[...].reshape(tile, 2 * sub).T[:sub]

    def spread_products(top, ps, pr, it):
        hi, lo = split(top)
        both = jnp.concatenate([hi, lo], axis=0)
        for turn in range(2):
            zd = other if turn == 0 else zh
            wide = jnp.dot(both, kh[zd, :, tile:], preferred_element_type=F32)
            wide = wide[:sub] + wide[sub:]
            wide = wide + jnp.dot(hi, kl[zd, :, tile:], preferred_element_type=F32)
            for q in range(1, nxy):
                ps[zd, q] = wide[:, (q - 1) * tile : q * tile]

            def one(k):
                q = lax.rem(xy + k, nxy)
                pl.when(q != 0)(
                    lambda: push(
                        ps.at[zd, q], pr.at[zd, xy], s_rs.at[it, turn], rs_sem.at[it, turn], plane(k)
                    )
                )

            each(nxy, one)

    take(tg0.at[pl.ds(0, ncol - 1)], col_sem.at[0])
    spread_products(upright(tg0), ps1, pr1, 0)

    def lay(vg, zd, q):
        hi, lo = split(vg[zd, q])
        vc[zd, :sub, q * tile : (q + 1) * tile] = hi
        vc[zd, sub:, q * tile : (q + 1) * tile] = lo

    def direct(first, last):
        cols = slice(first * tile, last * tile)
        total = jnp.zeros((tile, 2 * sub), F32)
        for zd in range(2):
            total = total + nt(kh[zd, :, cols], vc[zd, :, cols])
            total = total + nt(kl[zd, :, cols], vc[zd, :, cols])
        return total

    def scatter_direct(total, ds, dr, n):
        total = total + pltpu.roll(total, sub, 1)
        ds[...] = total.reshape(ds.shape)
        dr[col] = ds[col]

        def one(k):
            at = lax.rem(col + k, ncol)
            push(ds.at[at], dr.at[col], s_col.at[n], col_sem.at[n], in_col(k))

        each(ncol, one)

    for b in range(band):

        @pl.when(row < b * ncol + col)
        def _(b=b):
            ktr[b] = k_ref[b]

        @pl.when(row == b * ncol + col)
        def _(b=b):
            ktr[b] = 0.5 * (k_ref[b] + k_ref[b].T)

        @pl.when(row > b * ncol + col)
        def _(b=b):
            take(ktr.at[b], kq.at[b])
            ktr[b] = ktr[b].T

        hi, lo = split(ktr[b])
        kh[b, :, :tile] = hi
        kl[b, :, :tile] = lo

    take(vg0.at[0, pl.ds(0, nxy - 1)], ag_sem.at[0, 0])
    take(vg0.at[0, pl.ds(0, nxy - 1)], ag_sem.at[0, 1])
    for zd in range(2):
        for q in range(nxy):
            lay(vg0, zd, q)
    scatter_direct(direct(0, nxy), ds1, dr1, 1)

    def plane_sum(ps, pr, zd):
        total = ps[zd, xy]
        pr[zd, xy] = total
        total = pr[zd, 0]
        for q in range(1, nxy):
            total = total + pr[zd, q]
        return total

    lower = xy != 0

    def plane_sums(ps, pr, zs, zr, it):
        @pl.when(lower)
        def _():
            take(pr.at[0, pl.ds(0, nxy - 1)], rs_sem.at[it, 0])
            zs[...] = plane_sum(ps, pr, other)
            push(zs, zr, s_one.at[1 + it], z_sem.at[1 + it], zpart)
            take(pr.at[0, pl.ds(0, nxy - 1)], rs_sem.at[it, 1])
            troot[1 + it] = plane_sum(ps, pr, zh)

    plane_sums(ps1, pr1, zs1, zr1, 0)

    def line_sum(ref, count):
        total = ref[0]
        for p in range(1, count):
            total = total + ref[p]
        return total

    take(dr1.at[pl.ds(0, ncol - 1)], col_sem.at[1])
    piece1 = line_sum(dr1, ncol)
    tg1[col] = piece1
    all_in_col(tg1.at[col], tg1.at[col], 2)

    def piece_tile(piece):
        return jnp.concatenate([piece, jnp.zeros((tile - piece.shape[0], tile), F32)], axis=0).T[:sub]

    @pl.when(lower)
    def _():
        take(zr1, z_sem.at[1])
        troot[1] = troot[1] + zr1[...]
        push(troot.at[1], vg1.at[zh, xy], s_one.at[3], z_sem.at[3], zpart)
        each(nxy, lambda k: push(troot.at[1], vg1.at[zh, xy], s_xy.at[2], ag_sem.at[1, 0], plane(k)))
        vg1[zh, xy] = troot[1]

    @pl.when(jnp.logical_not(lower))
    def _():
        troot[1] = jnp.zeros((sub, tile), F32)
        troot[2] = jnp.zeros((sub, tile), F32)

    share = gs.shape[2]

    def gram_out(both, it):
        gram = nt_high(both, both)
        packed = jnp.concatenate([gram[: sub // 2], gram[sub // 2 :]], axis=1)
        for p in range(nxy):
            gs[it, p] = packed[p * share : (p + 1) * share]
        gr[it, xy] = gs[it, xy]

        def one(k):
            q = lax.rem(xy + k, nxy)
            push(gs.at[it, q], gr.at[it, xy], s_g.at[it, 0], g_sem.at[it, 0], plane(k))

        each(nxy, one)

    def gram_line(it):
        take(gr.at[it, pl.ds(0, nxy - 1)], g_sem.at[it, 0])
        gp[it] = line_sum(gr.at[it], nxy)
        gz[it, member] = gp[it]
        each(
            nline,
            lambda k: push(
                gp.at[it], gz.at[it, member], s_g.at[it, 1], g_sem.at[it, 1], in_line(k)
            ),
        )

    def gram_back(it):
        take(gz.at[it, pl.ds(0, nline - 1)], g_sem.at[it, 1])
        gq[it] = line_sum(gz.at[it], nline)
        ga[it, xy] = gq[it]
        each(
            nxy,
            lambda k: push(gq.at[it], ga.at[it, xy], s_g.at[it, 2], g_sem.at[it, 2], plane(k)),
        )

    def gram_in(it):
        take(ga.at[it, pl.ds(0, nxy - 1)], g_sem.at[it, 2])
        packed = jnp.concatenate([ga[it, p] for p in range(nxy)], axis=0)
        gram = jnp.concatenate([packed[:, :sub], packed[:, sub:]], axis=0)
        return gram / order

    gram_out(jnp.concatenate([troot[1], piece_tile(piece1)], axis=1), 0)

    take(tg1.at[pl.ds(0, ncol - 1)], col_sem.at[2])
    top = upright(tg1)

    @pl.when(is_root)
    def _():
        troot[0] = top
        push(troot.at[0], vg1.at[home, 0], s_top.at[1], top_sem.at[home], zpart)
        each(
            nxy,
            lambda k: push(troot.at[0], vg1.at[home, 0], s_top.at[0], top_sem.at[home], plane(k)),
        )
        vg1[home, 0] = top

    spread_products(top, ps2, pr2, 1)

    @pl.when(lower)
    def _():
        take(vg1.at[other, xy], z_sem.at[3])
        each(
            nxy,
            lambda k: push(
                vg1.at[other, xy], vg1.at[other, xy], s_xy.at[3], ag_sem.at[1, 1], plane(k)
            ),
        )

    root_part = col == lax.rem(row + 1 - 2 * zh, ncol)

    @pl.when(root_part)
    def _():
        take(vg1.at[home, 0], top_sem.at[home])
        each(
            nxy,
            lambda k: push(
                vg1.at[home, 0], vg1.at[home, 0], s_top.at[0], top_sem.at[home], plane(k)
            ),
        )

    gram_line(0)

    def take_tiles(ref, sem):
        pl.when(lower)(lambda: take(ref.at[0, pl.ds(0, nxy - 2)], sem))
        pl.when(jnp.logical_not(lower))(lambda: take(ref.at[0, pl.ds(0, nxy - 1)], sem))

    take_tiles(vg1, ag_sem.at[1, 0])
    take_tiles(vg1, ag_sem.at[1, 1])
    for zd in range(2):
        for q in range(1, nxy):
            lay(vg1, zd, q)
    partial = direct(1, nxy)
    for b in range(band):
        mine = jnp.logical_and(home == b, jnp.logical_or(is_root, root_part))
        pl.when(jnp.logical_not(mine))(functools.partial(lambda b: take(vg1.at[b, 0], top_sem.at[b]), b))
        lay(vg1, b, 0)
    scatter_direct(partial + direct(0, 1), ds2, dr2, 3)

    gram_back(0)
    plane_sums(ps2, pr2, zs2, zr2, 1)
    first = factorize(gram_in(0))
    back = first[:, sub:]

    take(dr2.at[pl.ds(0, ncol - 1)], col_sem.at[3])
    hp[...] = line_sum(dr2, ncol)

    @pl.when(self_held)
    def _():
        hz[col] = hp[...]

    @pl.when(jnp.logical_not(self_held))
    def _():
        push(hp, hz.at[col], s_h.at[1], hz_sem.at[0], holder())

    @pl.when(lower)
    def _():
        take(zr2, z_sem.at[2])
        troot[2] = troot[2] + zr2[...]

    both = jnp.concatenate([troot[2], piece_tile(hp[...])], axis=1)
    both = jnp.dot(back, both, precision=HI, preferred_element_type=F32)
    gram_out(both, 1)
    troot[3] = both[:, :tile]
    gram_line(1)

    @pl.when(holds)
    def _():
        pl.when(self_held)(lambda: take(hz.at[pl.ds(0, ncol - 1)], hz_sem.at[0]))
        pl.when(jnp.logical_not(self_held))(lambda: take(hz, hz_sem.at[0]))
        troot[3] = jnp.dot(back, upright(hz), precision=HI, preferred_element_type=F32)

    gram_back(1)
    second = factorize(gram_in(1))
    out_ref[...] = jnp.dot(second[:, sub:], troot[3], precision=HI, preferred_element_type=F32)
    keep = lax.broadcasted_iota(jnp.int32, (sub, sub), 0) >= lax.broadcasted_iota(
        jnp.int32, (sub, sub), 1
    )
    square = jnp.concatenate([second, second], axis=0).T[:sub, :sub]
    chol_ref[...] = jnp.where(keep, square, 0.0)

    many = nxy - 1
    take(v_ref, s_one.at[0])
    take(vg0.at[0, pl.ds(0, many)], s_xy.at[0])
    take(vg0.at[0, pl.ds(0, many)], s_xy.at[1])
    for b in range(band):
        pl.when(row < b * ncol + col)(
            functools.partial(lambda b: take(k_ref.at[b], s_one.at[4 + b]), b)
        )

    @pl.when(holds)
    def _():
        pl.when(self_held)(lambda: take(hs.at[pl.ds(0, ncol - 1)], s_h.at[0]))
        pl.when(jnp.logical_not(self_held))(lambda: take(hs, s_h.at[0]))

    pl.when(jnp.logical_not(self_held))(lambda: take(hp, s_h.at[1]))
    for n in range(4):
        take(tg0.at[pl.ds(0, ncol - 1)], s_col.at[n])
    for it in range(2):
        for turn in range(2):
            pl.when(lower)(lambda: take(pr1.at[0, pl.ds(0, many - 1)], s_rs.at[it, turn]))
            pl.when(jnp.logical_not(lower))(lambda: take(pr1.at[0, pl.ds(0, many)], s_rs.at[it, turn]))
        take(gs.at[it, pl.ds(0, many)], s_g.at[it, 0])
        take(gz.at[it, pl.ds(0, nline - 1)], s_g.at[it, 1])
        take(gs.at[it, pl.ds(0, many)], s_g.at[it, 2])

    @pl.when(lower)
    def _():
        take(zs1, s_one.at[1])
        take(zs2, s_one.at[2])
        take(zs1, s_one.at[3])
        take(vg1.at[0, pl.ds(0, many)], s_xy.at[2])
        take(vg1.at[0, pl.ds(0, many)], s_xy.at[3])

    @pl.when(is_root)
    def _():
        take(zs1, s_top.at[1])
        take(vg1.at[0, pl.ds(0, many)], s_top.at[0])

    @pl.when(root_part)
    def _():
        take(vg1.at[0, pl.ds(0, many)], s_top.at[0])


def per_device(nrow, ncol, kernel_tiles, basis):
    tiles, tile = kernel_tiles.shape[2], kernel_tiles.shape[3]
    sub = basis.shape[0]
    nxy, band, nline = nrow // 2, nrow // ncol, 2 * ncol
    planes = (2, nxy, sub, tile)
    pieces = (ncol, tile // ncol, 2 * sub)
    share = sub // 2 // nxy
    wide = 2 * sub
    vmem = lambda shape, kind=F32: pltpu.VMEM(shape, kind)
    dma = lambda *shape: pltpu.SemaphoreType.DMA(shape)
    scratch = [
        vmem((2, tile, nxy * tile), BF16), vmem((2, tile, nxy * tile), BF16),
        vmem((2, 2 * sub, nxy * tile), BF16), vmem((band, tile, tile)),
        vmem(planes), vmem(planes), vmem(planes), vmem(planes), vmem(planes), vmem(planes),
        vmem((sub, tile)), vmem((sub, tile)), vmem((sub, tile)), vmem((sub, tile)),
        vmem((4, sub, tile)),
        vmem(pieces), vmem(pieces), vmem(pieces), vmem(pieces),
        vmem(pieces[1:]), vmem(pieces), vmem(pieces), vmem(pieces), vmem(pieces[1:]), vmem(pieces),
        vmem((2, nxy, share, wide)), vmem((2, nxy, share, wide)), vmem((2, share, wide)),
        vmem((2, nline, share, wide)), vmem((2, share, wide)), vmem((2, nxy, share, wide)),
        dma(band), dma(1), dma(4), dma(2, 2), dma(2, 2), dma(4), dma(band), dma(1), dma(2, 3),
        dma(4 + band), dma(4), dma(2, 2), dma(4), dma(2), dma(2, 3), dma(2),
    ]
    flops = 2 * 3 * 4 * tiles * tile * tile * sub
    out, chol = pl.pallas_call(
        functools.partial(kernel, nrow, ncol),
        out_shape=(
            jax.ShapeDtypeStruct((sub, tile), F32),
            jax.ShapeDtypeStruct((sub, sub), F32),
        ),
        in_specs=[pl.BlockSpec(memory_space=pltpu.VMEM)] * 2,
        out_specs=(pl.BlockSpec(memory_space=pltpu.VMEM),) * 2,
        scratch_shapes=scratch,
        compiler_params=pltpu.CompilerParams(
            collective_id=0, has_side_effects=True, vmem_limit_bytes=40 * 1024 * 1024
        ),
        cost_estimate=pl.CostEstimate(
            flops=flops, bytes_accessed=4 * tiles * tile * tile, transcendentals=0
        ),
        name="subspace",
    )(kernel_tiles[0, 0], basis.reshape(sub, tile))
    return out.reshape(sub, 1, 1, tile), chol


def solution(mesh):
    nrow, ncol = mesh.shape["row"], mesh.shape["col"]
    return jax.shard_map(
        functools.partial(per_device, nrow, ncol),
        mesh=mesh,
        in_specs=(P("row", "col", None, None, None), P(None, "row", "col", None)),
        out_specs=(P(None, "row", "col", None), P()),
        check_vma=False,
    )
```

time: 1680 us -> 126 us (0.07)
  waiting for transfers between devices: 1360 us -> 0 us
  blocking collectives: 246 us -> 0 us
  Pallas kernels: 0 us -> 121 us
  matrix products: 26.3 us -> 0 us
  other arithmetic: 24.8 us -> 0 us
    reduce_scatter x2 -> x0, waiting for transfers between devices: 555 us -> none  [per_device(): lax.psum_scatter(tile_terms, 'row', scatter_dimension=0, tiled=True)]
    all_gather x4 -> x0, waiting for transfers between devices: 456 us -> none  [the longest x2 229 us: per_device(): lax.all_gather(total_direct[:, None, :], 'row', axis=1, tiled=True)]
    psum x2 -> x0, waiting for transfers between devices: 349 us -> none  [per_device(): total_direct, band_vector = lax.psum((direct, own_tile), 'col')]
    psum x2 -> x0, blocking collectives: 246 us -> none  [per_device(): gram_sum = lax.psum(gram_part, ('row', 'col')) / order_total]
    pallas_call x0 -> x1, Pallas kernels: none -> 121 us  [per_device(): pl.pallas_call(functools.partial(kernel, nrow, ncol), out_shape=(jax.Shap...]
    another operation x10 -> x0, other arithmetic: 24.8 us -> none  [the longest x6 13 us: per_device(): cholesky_factor = jnp.linalg.cholesky(gram_sum)]
    dot_general x12 -> x0, matrix products: 23 us -> none  [the longest x2 5.99 us: per_device(): jnp.einsum('bts,kt->bks', kernel_local, band_vector, precision=highest)]
  transfers between devices with their start and end apart: 8 -> 0, of which waited for: 8 -> 0; matrix products, arithmetic and copies ran while one was open for 1% -> 0% of each run, Pallas kernels for 0% -> 0%
where the time goes in v1:
time: 126 us
  Pallas kernels  121 us (96%)
  local copies, waits for them, and re-layouts  3.57 us (3%)
    pallas_call x1, Pallas kernels, per_device(): pl.pallas_call(functools.partial(kernel, nrow, ncol), out_shape=(jax.Shap...  121 us
    unnamed x6, local copies, waits for them, and re-layouts  3.57 us

profile of v1, /device:TPU:1, one launch (start us, length us, event | category | flops | bytes accessed | tf_op | source)
XLA Modules:
  0.0 125.6 jit_solution(13776186326565180798)
XLA Ops:
  0.6 0.0 copy-start
  0.6 1.6 %copy-done = f32[1,1,32,128,128]{4,3,2,1,0:T(8,128)S(1)} copy-done((f32[1,1,32,128,128]{4,3,2,1,0:T(8,128)S(1)}, f32[1,1,32,128,128]{4,3,2,1,0:T(8,128)}, u32[]{:S(2)}) %copy-start) | copy-done | bytes 2097176
  2.2 0.0 copy-start.1
  2.2 0.8 copy-done.1
  3.0 121.4 %subspace.1 = (f32[64,128]{1,0:T(8,128)S(1)}, f32[64,64]{1,0:T(8,128)S(1)}) custom-call(f32[32,128,128]{2,1,0:T(8,128)S(1)} %bitcast.6, f32[64,128]{1,0:T(8,128)S(1)} %bitcast.7), custom_call_target="tpu_custom_call" | custom-call | flops 805306368 | bytes 2097152 | tf_op jit(solution)/shard_map/subspace/pallas_call | solution.py:524
  124.4 0.6 copy.7
  125.0 0.6 copy.8
Async XLA Ops:
  0.6 1.6 %copy-start = (f32[1,1,32,128,128]{4,3,2,1,0:T(8,128)S(1)}, f32[1,1,32,128,128]{4,3,2,1,0:T(8,128)}, u32[]{:S(2)}) copy-start(f32[1,1,32,128,128]{4,3,2,1,0:T(8,128)} %param.2) | copy-start | bytes 6291460
  2.2 0.8 copy-start.1

commit v2 on v1

v2 whole, which is shorter than its diff:
```python
import functools

import jax
import jax.numpy as jnp
from jax import lax
from jax.experimental import pallas as pl
from jax.experimental.pallas import tpu as pltpu
from jax.sharding import PartitionSpec as P

MESH = pl.DeviceIdType.MESH
HI = lax.Precision.HIGHEST
F32 = jnp.float32
BF16 = jnp.bfloat16


def split(x):
    hi = x.astype(BF16)
    return hi, (x - hi.astype(F32)).astype(BF16)


def nt(a, b):
    return lax.dot_general(a, b, (((1,), (1,)), ((), ())), preferred_element_type=F32)


def nt_high(a, b):
    return lax.dot_general(
        a, b, (((1,), (1,)), ((), ())), precision=HI, preferred_element_type=F32
    )


def lane(block, k):
    return jnp.broadcast_to(block[:, k : k + 1], (8, block.shape[1]))


def line(block, j):
    return jnp.broadcast_to(block[j : j + 1], (8, block.shape[1]))


def factorize(gram):
    n = gram.shape[0]
    eye = (
        lax.broadcasted_iota(jnp.int32, (n, n), 0) == lax.broadcasted_iota(jnp.int32, (n, n), 1)
    ).astype(F32)
    full = jnp.concatenate([gram, eye], axis=1)
    blocks = [full[8 * j : 8 * j + 8] for j in range(n // 8)]
    at_row = lax.broadcasted_iota(jnp.int32, (8, 2 * n), 0)
    for at in range(n // 8):
        block, first = blocks[at], 8 * at
        columns = [lane(block, first + i) for i in range(8)]
        corner = [[line(columns[i], j) for i in range(j + 1)] for j in range(8)]
        rows = [line(block, j) for j in range(8)]
        inverse = [None] * 8
        ratio = [[None] * 8 for _ in range(8)]
        for i in range(8):
            inverse[i] = 1.0 / corner[i][i]
            for j in range(i + 1, 8):
                ratio[j][i] = corner[j][i] * inverse[i]
            for j in range(i + 1, 8):
                for m in range(i + 1, j + 1):
                    corner[j][m] = corner[j][m] - ratio[j][i] * corner[m][i]
                rows[j] = rows[j] - ratio[j][i] * rows[i]
        scaled = [rows[i] * inverse[i] for i in range(8)]
        for i in range(6, -1, -1):
            for m in range(i + 1, 8):
                scaled[i] = scaled[i] - ratio[m][i] * scaled[m]
        for j in range(at + 1, n // 8):
            terms = [lane(blocks[j], first + i) * scaled[i] for i in range(8)]
            while len(terms) > 1:
                terms = [terms[i] + terms[i + 1] for i in range(0, len(terms), 2)]
            blocks[j] = blocks[j] - terms[0]
        done = rows[0]
        for j in range(1, 8):
            done = jnp.where(at_row == j, rows[j], done)
        blocks[at] = done
    full = jnp.concatenate(blocks, axis=0)
    diagonal = jnp.sum(full[:, :n] * eye, axis=1, keepdims=True)
    return full * lax.rsqrt(diagonal)


def kernel(nrow, ncol, k_ref, v_ref, out_ref, chol_ref, *scratch):
    (
        kv, kh, kl, vc, ktr, vg0, vg1, vtop, ps1, ps2, r1, s2, r2, zs, zr, mine,
        ds1, dr1, ds2, dr2, hs, tp0, tg0, tg1, hp, hz,
        gs, gr, gp, gz, gq, ga,
        ld, kq, tps, z_sem, ag_sem, rs_sem, col_sem, top_sem, hz_sem, g_sem,
        s_one, s_ag, s_rs, s_col, s_top, s_g, s_h,
    ) = scratch
    nxy = nrow // 2
    nline = 2 * ncol
    band = nrow // ncol
    row, col = lax.axis_index("row"), lax.axis_index("col")
    xy, zh = row // 2, row % 2
    side = ps1.shape[1]
    y, x = xy // side, lax.rem(xy, side)
    other = 1 - zh
    sub, tile = v_ref.shape
    order = nrow * ncol * tile
    member = zh * ncol + col
    home = row // ncol
    is_root = col == row % ncol
    holds = row < band
    self_held = jnp.logical_and(row == home, is_root)
    zpart = (xy * 2 + other, col)

    def plane(k):
        return (lax.rem(xy + k, nxy) * 2 + zh, col)

    def along(axis, k):
        if axis == 0:
            return ((lax.rem(y + k, side) * side + x) * 2 + zh, col)
        return ((y * side + lax.rem(x + k, side)) * 2 + zh, col)

    def in_col(k):
        return (row, lax.rem(col + k, ncol))

    def in_line(k):
        at = lax.rem(member + k, nline)
        return (xy * 2 + at // ncol, lax.rem(at, ncol))

    def mirror(b):
        return (b * ncol + col, lax.rem(row, ncol))

    def holder():
        return (home, lax.rem(row, ncol))

    def held_member(p):
        return (row * ncol + col, p)

    def each(n, body, start=1):
        def step(k, carry):
            body(k)
            return carry

        lax.fori_loop(start, n, step, 0)

    def push(src, dst, s, r, where):
        pltpu.make_async_remote_copy(
            src_ref=src, dst_ref=dst, send_sem=s, recv_sem=r, device_id=where, device_id_type=MESH
        ).start()

    def take(ref, sem):
        pltpu.make_async_copy(ref, ref, sem).wait()

    loads = ld.shape[0] - 1
    chunk = nrow // loads

    def load(n):
        part = pl.ds(n * chunk, chunk)
        return pltpu.make_async_copy(k_ref.at[part], kv.at[part], ld.at[n])

    load_v = pltpu.make_async_copy(v_ref, vg0.at[zh, y, x], ld.at[loads])
    load_v.start()
    for n in range(loads):
        load(n).start()

    bar = pltpu.get_barrier_semaphore()

    def greet(where):
        pl.semaphore_signal(bar, inc=1, device_id=where, device_id_type=MESH)

    each(nline, lambda k: greet(in_line(k)))
    each(nxy, lambda k: greet(plane(k)))
    for b in range(band):
        pl.when(b * ncol + col != row)(functools.partial(lambda b: greet(mirror(b)), b))
    pl.when(jnp.logical_not(self_held))(lambda: greet(holder()))

    def held_one(p, act):
        same = jnp.logical_and(row * ncol + col == row, p == col)
        pl.when(jnp.logical_not(same))(act)

    @pl.when(holds)
    def _():
        each(ncol, lambda p: held_one(p, lambda: greet(held_member(p))), 0)

    for zd in range(2):
        ps1[zd, 0, 0] = jnp.zeros((sub, tile), F32)
        ps2[zd, 0, 0] = jnp.zeros((sub, tile), F32)
    for n in range(loads):
        load(n).wait()
        for at in range(max(n * chunk, 2), (n + 1) * chunk):
            q, zd = divmod(at, 2)
            hi, lo = split(kv[at])
            kh[zd, :, q * tile : (q + 1) * tile] = hi
            kl[zd, :, q * tile : (q + 1) * tile] = lo
    load_v.wait()

    @pl.when(holds)
    def _():
        tile0 = vg0[zh, y, x]
        hs[...] = jnp.concatenate([tile0, tile0], axis=0).T.reshape(hs.shape)

    greeted = (nxy - 1) + (nline - 1) + band - is_root.astype(jnp.int32)
    greeted = greeted + jnp.where(self_held, 0, 1)
    greeted = greeted + jnp.where(holds, ncol, 0) - jnp.where(self_held, 1, 0)
    pl.semaphore_wait(bar, greeted)

    @pl.when(holds)
    def _():
        each(
            ncol,
            lambda p: held_one(
                p, lambda: push(hs.at[p], tp0, s_h.at[0], tps.at[0], held_member(p))
            ),
            0,
        )

    push(v_ref, vg0.at[zh, y, x], s_one.at[0], z_sem.at[0], zpart)

    low, high = pl.ds(0, sub // 2), pl.ds(sub // 2, sub // 2)

    def gather_start(src, vg, unit, zd):
        each(
            side,
            lambda k: push(
                src.at[low], vg.at[zd, y, x, low], s_ag.at[unit, 0, 0], ag_sem.at[unit, 0, 0], along(1, k)
            ),
        )
        each(
            side,
            lambda k: push(
                src.at[high], vg.at[zd, y, x, high], s_ag.at[unit, 1, 0], ag_sem.at[unit, 1, 0], along(0, k)
            ),
        )

    def gather_turn(vg, unit, zd):
        take(vg.at[0, 0, pl.ds(0, side - 1), low], ag_sem.at[unit, 0, 0])
        part = vg.at[zd, y, :, low]
        each(side, lambda k: push(part, part, s_ag.at[unit, 0, 1], ag_sem.at[unit, 0, 1], along(0, k)))
        take(vg.at[0, 0, pl.ds(0, side - 1), low], ag_sem.at[unit, 1, 0])
        rest = vg.at[zd, :, x, high]
        each(side, lambda k: push(rest, rest, s_ag.at[unit, 1, 1], ag_sem.at[unit, 1, 1], along(1, k)))

    def gather_end(vg, unit):
        take(vg.at[0, pl.ds(0, side - 1), :, low], ag_sem.at[unit, 0, 1])
        take(vg.at[0, pl.ds(0, side - 1), :, low], ag_sem.at[unit, 1, 1])

    gather_start(v_ref, vg0, 0, zh)
    for b in range(band):

        @pl.when(row < b * ncol + col)
        def _(b=b):
            push(kv.at[b], ktr.at[home], s_one.at[4 + b], kq.at[home], mirror(b))

    def to_plane(src, dst, s, r):
        each(nxy, lambda k: push(src, dst, s, r, plane(k)))

    def upright(pieces):
        return pieces[...].reshape(tile, 2 * sub).T[:sub]

    def spread_products(top, ps, it, turn):
        hi, lo = top
        zd = other if turn == 0 else zh
        wide = jnp.dot(jnp.concatenate([hi, lo], axis=0), kh[zd, :, tile:], preferred_element_type=F32)
        wide = wide[:sub] + wide[sub:]
        wide = wide + jnp.dot(hi, kl[zd, :, tile:], preferred_element_type=F32)
        for q in range(1, nxy):
            ps[zd, q // side, q % side] = wide[:, (q - 1) * tile : q * tile]
        for half, (axis, rows) in enumerate(((0, low), (1, high))):

            def one(k, half=half, axis=axis, rows=rows):
                at = lax.rem((x if axis else y) + k, side)
                push(
                    ps.at[zd, :, at, rows] if axis else ps.at[zd, at, :, rows],
                    r1.at[it, turn, half, x if axis else y],
                    s_rs.at[it, turn, half, 0],
                    rs_sem.at[it, turn, half, 0],
                    along(axis, k),
                )

            each(side, one)

    def total_of(ref):
        total = ref[0]
        for n in range(1, side):
            total = total + ref[n]
        return total

    def sum_turn(ps, it, turn):
        zd = other if turn == 0 else zh
        for half, (axis, rows) in enumerate(((0, low), (1, high))):
            take(r1.at[0, 0, 0, pl.ds(0, side - 1)], rs_sem.at[it, turn, half, 0])
            r1[it, turn, half, x if axis else y] = ps[zd, :, x, rows] if axis else ps[zd, y, :, rows]
            s2[it, turn, half] = total_of(r1.at[it, turn, half])
            here = y if axis else x
            r2[it, turn, half, here] = s2[it, turn, half, here]

            def one(k, half=half, axis=axis, here=here):
                push(
                    s2.at[it, turn, half, lax.rem(here + k, side)],
                    r2.at[it, turn, half, here],
                    s_rs.at[it, turn, half, 1],
                    rs_sem.at[it, turn, half, 1],
                    along(1 - axis, k),
                )

            each(side, one)

    def sum_end(it, turn):
        halves = []
        for half in range(2):
            take(r2.at[0, 0, 0, pl.ds(0, side - 1)], rs_sem.at[it, turn, half, 1])
            halves.append(total_of(r2.at[it, turn, half]))
        return jnp.concatenate(halves, axis=0)

    def lay(vg, zd, first):
        for q in range(first, nxy):
            hi, lo = split(vg[zd, q // side, q % side])
            vc[zd, :sub, q * tile : (q + 1) * tile] = hi
            vc[zd, sub:, q * tile : (q + 1) * tile] = lo

    def direct(zd, first, last):
        cols = slice(first * tile, last * tile)
        return nt(kh[zd, :, cols], vc[zd, :, cols]) + nt(kl[zd, :, cols], vc[zd, :, cols])

    def scatter_direct(total, ds, dr, n):
        total = total + pltpu.roll(total, sub, 1)
        ds[...] = total.reshape(ds.shape)
        dr[col] = ds[col]

        def one(k):
            at = lax.rem(col + k, ncol)
            push(ds.at[at], dr.at[col], s_col.at[n], col_sem.at[n], in_col(k))

        each(ncol, one)

    def line_sum(ref, count):
        total = ref[0]
        for p in range(1, count):
            total = total + ref[p]
        return total

    def piece_tile(piece):
        return jnp.concatenate([piece, jnp.zeros((tile - piece.shape[0], tile), F32)], axis=0).T[:sub]

    share = gs.shape[2]

    def gram_out(both, it):
        gram = nt_high(both, both)
        packed = jnp.concatenate([gram[: sub // 2], gram[sub // 2 :]], axis=1)
        for p in range(nxy):
            gs[it, p] = packed[p * share : (p + 1) * share]
        gr[it, xy] = gs[it, xy]

        def one(k):
            q = lax.rem(xy + k, nxy)
            push(gs.at[it, q], gr.at[it, xy], s_g.at[it, 0], g_sem.at[it, 0], plane(k))

        each(nxy, one)

    def gram_line(it):
        take(gr.at[it, pl.ds(0, nxy - 1)], g_sem.at[it, 0])
        gp[it] = line_sum(gr.at[it], nxy)
        gz[it, member] = gp[it]
        each(
            nline,
            lambda k: push(
                gp.at[it], gz.at[it, member], s_g.at[it, 1], g_sem.at[it, 1], in_line(k)
            ),
        )

    def gram_back(it):
        take(gz.at[it, pl.ds(0, nline - 1)], g_sem.at[it, 1])
        gq[it] = line_sum(gz.at[it], nline)
        ga[it, xy] = gq[it]
        to_plane(gq.at[it], ga.at[it, xy], s_g.at[it, 2], g_sem.at[it, 2])

    def gram_in(it):
        take(ga.at[it, pl.ds(0, nxy - 1)], g_sem.at[it, 2])
        packed = jnp.concatenate([ga[it, p] for p in range(nxy)], axis=0)
        gram = jnp.concatenate([packed[:, :sub], packed[:, sub:]], axis=0)
        return gram / order

    gather_turn(vg0, 0, zh)

    take(vg0.at[other, y, x], z_sem.at[0])
    gather_start(vg0.at[other, y, x], vg0, 1, other)

    @pl.when(self_held)
    def _():
        tp0[...] = hs[col]

    @pl.when(jnp.logical_not(self_held))
    def _():
        take(tp0, tps.at[0])

    tg0[col] = tp0[...]
    each(ncol, lambda k: push(tp0, tg0.at[col], s_col.at[3], col_sem.at[3], in_col(k)))
    gather_turn(vg0, 1, other)

    for b in range(band):

        @pl.when(row < b * ncol + col)
        def _(b=b):
            ktr[b] = kv[b]

        @pl.when(row == b * ncol + col)
        def _(b=b):
            ktr[b] = 0.5 * (kv[b] + kv[b].T)

        @pl.when(row > b * ncol + col)
        def _(b=b):
            take(ktr.at[b], kq.at[b])
            ktr[b] = ktr[b].T

        hi, lo = split(ktr[b])
        kh[b, :, :tile] = hi
        kl[b, :, :tile] = lo

    gather_end(vg0, 0)
    lay(vg0, zh, 0)
    total = direct(zh, 0, nxy)

    take(tg0.at[pl.ds(0, ncol - 1)], col_sem.at[3])
    top = split(upright(tg0))
    spread_products(top, ps1, 0, 0)

    gather_end(vg0, 1)
    lay(vg0, other, 0)
    scatter_direct(total + direct(other, 0, nxy), ds1, dr1, 0)

    spread_products(top, ps1, 0, 1)
    sum_turn(ps1, 0, 0)

    take(dr1.at[pl.ds(0, ncol - 1)], col_sem.at[0])
    piece1 = line_sum(dr1, ncol)
    tg1[col] = piece1
    each(ncol, lambda k: push(tg1.at[col], tg1.at[col], s_col.at[1], col_sem.at[1], in_col(k)))

    sum_turn(ps1, 0, 1)
    for turn in range(2):
        zs[turn] = sum_end(0, turn)
        push(zs.at[turn], zr.at[turn], s_one.at[1 + turn], z_sem.at[1 + turn], zpart)

    take(tg1.at[pl.ds(0, ncol - 1)], col_sem.at[1])
    top = upright(tg1)

    @pl.when(is_root)
    def _():
        mine[0] = top
        push(mine.at[0], vtop.at[home], s_top.at[1], top_sem.at[home], zpart)
        to_plane(mine.at[0], vtop.at[home], s_top.at[0], top_sem.at[home])
        vtop[home] = top

    parts = split(top)
    spread_products(parts, ps2, 1, 0)

    take(zr.at[0], z_sem.at[1])
    mine[1] = zs[1] + zr[0]
    vg1[zh, y, x] = mine[1]
    gram_out(jnp.concatenate([mine[1], piece_tile(piece1)], axis=1), 0)
    gather_start(mine.at[1], vg1, 2, zh)
    spread_products(parts, ps2, 1, 1)
    take(zr.at[1], z_sem.at[2])
    mine[2] = zs[0] + zr[1]
    vg1[other, y, x] = mine[2]
    gather_start(mine.at[2], vg1, 3, other)

    sum_turn(ps2, 1, 0)
    gather_turn(vg1, 2, zh)
    gram_line(0)
    gather_turn(vg1, 3, other)
    zs[2] = sum_end(1, 0)
    push(zs.at[2], zr.at[2], s_one.at[3], z_sem.at[3], zpart)

    root_part = col == lax.rem(row + 1 - 2 * zh, ncol)

    @pl.when(root_part)
    def _():
        take(vtop.at[home], top_sem.at[home])
        to_plane(vtop.at[home], vtop.at[home], s_top.at[0], top_sem.at[home])

    sum_turn(ps2, 1, 1)
    gather_end(vg1, 2)
    lay(vg1, zh, 1)
    total = direct(zh, 1, nxy)
    gather_end(vg1, 3)
    lay(vg1, other, 1)
    total = total + direct(other, 1, nxy)
    gram_back(0)
    for b in range(band):
        own = jnp.logical_and(home == b, jnp.logical_or(is_root, root_part))
        pl.when(jnp.logical_not(own))(functools.partial(lambda b: take(vtop.at[b], top_sem.at[b]), b))
        hi, lo = split(vtop[b])
        vc[b, :sub, :tile] = hi
        vc[b, sub:, :tile] = lo
        total = total + direct(b, 0, 1)
    scatter_direct(total, ds2, dr2, 2)

    rest = sum_end(1, 1)
    first = factorize(gram_in(0))
    back = first[:, sub:]

    take(dr2.at[pl.ds(0, ncol - 1)], col_sem.at[2])
    hp[...] = line_sum(dr2, ncol)

    @pl.when(self_held)
    def _():
        hz[col] = hp[...]

    @pl.when(jnp.logical_not(self_held))
    def _():
        push(hp, hz.at[col], s_h.at[1], hz_sem.at[0], holder())

    take(zr.at[2], z_sem.at[3])
    both = jnp.concatenate([rest + zr[2], piece_tile(hp[...])], axis=1)
    both = jnp.dot(back, both, precision=HI, preferred_element_type=F32)
    gram_out(both, 1)
    mine[3] = both[:, :tile]
    gram_line(1)

    @pl.when(holds)
    def _():
        pl.when(self_held)(lambda: take(hz.at[pl.ds(0, ncol - 1)], hz_sem.at[0]))
        pl.when(jnp.logical_not(self_held))(lambda: take(hz, hz_sem.at[0]))
        mine[3] = jnp.dot(back, upright(hz), precision=HI, preferred_element_type=F32)

    gram_back(1)
    second = factorize(gram_in(1))
    out_ref[...] = jnp.dot(second[:, sub:], mine[3], precision=HI, preferred_element_type=F32)
    keep = lax.broadcasted_iota(jnp.int32, (sub, sub), 0) >= lax.broadcasted_iota(
        jnp.int32, (sub, sub), 1
    )
    square = jnp.concatenate([second, second], axis=0).T[:sub, :sub]
    chol_ref[...] = jnp.where(keep, square, 0.0)

    many = nxy - 1
    take(mine.at[0], s_one.at[0])
    for n in range(3):
        take(zs.at[n], s_one.at[1 + n])
    for b in range(band):
        pl.when(row < b * ncol + col)(
            functools.partial(lambda b: take(kv.at[b], s_one.at[4 + b]), b)
        )
    for unit in range(4):
        for half in range(2):
            take(vg0.at[0, 0, pl.ds(0, side - 1), low], s_ag.at[unit, half, 0])
            take(vg0.at[0, pl.ds(0, side - 1), :, low], s_ag.at[unit, half, 1])

    @pl.when(holds)
    def _():
        pl.when(self_held)(lambda: take(hs.at[pl.ds(0, ncol - 1)], s_h.at[0]))
        pl.when(jnp.logical_not(self_held))(lambda: take(hs, s_h.at[0]))

    pl.when(jnp.logical_not(self_held))(lambda: take(hp, s_h.at[1]))
    for n in range(4):
        take(tg1.at[pl.ds(0, ncol - 1)], s_col.at[n])
    for it in range(2):
        for turn in range(2):
            for half in range(2):
                take(r1.at[0, 0, 0, pl.ds(0, side - 1)], s_rs.at[it, turn, half, 0])
                take(r2.at[0, 0, 0, pl.ds(0, side - 1)], s_rs.at[it, turn, half, 1])
        take(gs.at[it, pl.ds(0, many)], s_g.at[it, 0])
        take(gz.at[it, pl.ds(0, nline - 1)], s_g.at[it, 1])
        take(gs.at[it, pl.ds(0, many)], s_g.at[it, 2])

    @pl.when(is_root)
    def _():
        take(mine.at[0], s_top.at[1])

    @pl.when(jnp.logical_or(is_root, root_part))
    def _():
        for n in range(side - 1):
            take(vg0.at[0, n], s_top.at[0])
        take(vg0.at[0, 0, pl.ds(0, side - 1)], s_top.at[0])


def per_device(nrow, ncol, kernel_tiles, basis):
    tiles, tile = kernel_tiles.shape[2], kernel_tiles.shape[3]
    sub = basis.shape[0]
    nxy, band, nline = nrow // 2, nrow // ncol, 2 * ncol
    pieces = (ncol, tile // ncol, 2 * sub)
    share = sub // 2 // nxy
    wide = 2 * sub
    vmem = lambda shape, kind=F32: pltpu.VMEM(shape, kind)
    dma = lambda *shape: pltpu.SemaphoreType.DMA(shape)
    side = 4 if nxy == 16 else 2
    halves = (2, 2, 2, side)
    half = (sub // 2, tile)
    planes = (2, side, nxy // side, sub, tile)
    scratch = [
        vmem((tiles, tile, tile)),
        vmem((2, tile, nxy * tile), BF16), vmem((2, tile, nxy * tile), BF16),
        vmem((2, 2 * sub, nxy * tile), BF16), vmem((band, tile, tile)),
        vmem(planes), vmem(planes), vmem((band, sub, tile)), vmem(planes), vmem(planes),
        vmem(halves + (side,) + half), vmem(halves + half), vmem(halves + half),
        vmem((3, sub, tile)), vmem((3, sub, tile)), vmem((4, sub, tile)),
        vmem(pieces), vmem(pieces), vmem(pieces), vmem(pieces),
        vmem(pieces), vmem(pieces[1:]), vmem(pieces), vmem(pieces), vmem(pieces[1:]), vmem(pieces),
        vmem((2, nxy, share, wide)), vmem((2, nxy, share, wide)), vmem((2, share, wide)),
        vmem((2, nline, share, wide)), vmem((2, share, wide)), vmem((2, nxy, share, wide)),
        dma(5), dma(band), dma(1), dma(4), dma(4, 2, 2), dma(2, 2, 2, 2), dma(4), dma(band), dma(1),
        dma(2, 3),
        dma(4 + band), dma(4, 2, 2), dma(2, 2, 2, 2), dma(4), dma(2), dma(2, 3), dma(2),
    ]
    flops = 2 * 3 * 4 * tiles * tile * tile * sub
    out, chol = pl.pallas_call(
        functools.partial(kernel, nrow, ncol),
        out_shape=(
            jax.ShapeDtypeStruct((sub, tile), F32),
            jax.ShapeDtypeStruct((sub, sub), F32),
        ),
        in_specs=[pl.BlockSpec(memory_space=pltpu.HBM)] * 2,
        out_specs=(pl.BlockSpec(memory_space=pltpu.VMEM),) * 2,
        scratch_shapes=scratch,
        compiler_params=pltpu.CompilerParams(
            collective_id=0, has_side_effects=True, vmem_limit_bytes=63 * 1024 * 1024
        ),
        cost_estimate=pl.CostEstimate(
            flops=flops, bytes_accessed=4 * tiles * tile * tile, transcendentals=0
        ),
        name="subspace",
    )(kernel_tiles[0, 0], basis.reshape(sub, tile))
    return out.reshape(sub, 1, 1, tile), chol


def solution(mesh):
    nrow, ncol = mesh.shape["row"], mesh.shape["col"]
    return jax.shard_map(
        functools.partial(per_device, nrow, ncol),
        mesh=mesh,
        in_specs=(P("row", "col", None, None, None), P(None, "row", "col", None)),
        out_specs=(P(None, "row", "col", None), P()),
        check_vma=False,
    )
```

time: 126 us -> 113 us (0.90)
  Pallas kernels: 121 us -> 109 us
    pallas_call x1, Pallas kernels: 121 us -> 109 us  [per_device(): pl.pallas_call(functools.partial(kernel, nrow, ncol), out_shape=(jax.Shap...]
    unnamed x6 -> x2, local copies, waits for them, and re-layouts: 3.57 us -> 2.75 us
where the time goes in v2:
time: 113 us
  Pallas kernels  109 us (96%)
  local copies, waits for them, and re-layouts  2.75 us (2%)
    pallas_call x1, Pallas kernels, per_device(): pl.pallas_call(functools.partial(kernel, nrow, ncol), out_shape=(jax.Shap...  109 us
    unnamed x2, local copies, waits for them, and re-layouts  2.75 us

profile of v2, /device:TPU:1, one launch (start us, length us, event | category | flops | bytes accessed | tf_op | source)
XLA Modules:
  0.0 112.6 jit_solution(13911856174228259333)
XLA Ops:
  0.6 109.2 %subspace.1 = (f32[64,128]{1,0:T(8,128)}, f32[64,64]{1,0:T(8,128)}) custom-call(f32[32,128,128]{2,1,0:T(8,128)} %bitcast.6, f32[64,128]{1,0:T(8,128)} %bitcast.7), custom_call_target="tpu_custom_call" | custom-call | flops 805306368 | bytes 2097152 | tf_op jit(solution)/shard_map/subspace/pallas_call | solution.py:596
  109.9 1.4 %copy.7 = f32[64,1,1,128]{3,2,1,0:T(1,128)} copy(f32[64,1,1,128]{3,2,1,0:T(1,128)} %bitcast.5) | data formatting | bytes 65536
  111.3 1.4 %copy.8 = f32[64,64]{1,0:T(8,128)} copy(f32[64,64]{1,0:T(8,128)} %get-tuple-element.11) | data formatting | bytes 32768

commit v3 on v2

--- a/solution.py
+++ b/solution.py
@@ -8,6 +8,15 @@
 from jax.sharding import PartitionSpec as P
 
 MESH = pl.DeviceIdType.MESH
+ORDER = (
+    "cut_kernel", "own_turn", "other_start", "top_pieces", "other_turn", "mirrored", "direct_own",
+    "spread_other", "direct_other", "spread_own", "turn_other", "direct_sum", "z_other", "turn_own", "z_own",
+    "top_tile", "spread_other1", "own_tile", "gram_start", "own_start1", "spread_own1", "other_start1",
+    "turn_other1", "own_turn1", "gram_line0", "other_turn1", "z_other1", "top_forward", "turn_own1",
+    "gram_back0", "direct_own1", "direct_other1", "direct_top1", "rest_own1", "factor0", "direct_sum1",
+)
+D_AG = (False, True, False, False)
+D_RS = ((True, True), (False, False))
 HI = lax.Precision.HIGHEST
 F32 = jnp.float32
 BF16 = jnp.bfloat16
@@ -77,9 +86,25 @@
     return full * lax.rsqrt(diagonal)
 
 
-def kernel(nrow, ncol, k_ref, v_ref, out_ref, chol_ref, *scratch):
+def unpacked(packed):
+    sub = packed.shape[1] // 2
+    return jnp.concatenate([packed[:, :sub], packed[:, sub:]], axis=0)
+
+
+def finish(order, gram_ref, last_ref, out_ref, chol_ref):
+    sub = last_ref.shape[0]
+    second = factorize(unpacked(gram_ref[...]) / order)
+    out_ref[...] = jnp.dot(second[:, sub:], last_ref[...], precision=HI, preferred_element_type=F32)
+    keep = lax.broadcasted_iota(jnp.int32, (sub, sub), 0) >= lax.broadcasted_iota(
+        jnp.int32, (sub, sub), 1
+    )
+    square = jnp.concatenate([second, second], axis=0).T[:sub, :sub]
+    chol_ref[...] = jnp.where(keep, square, 0.0)
+
+
+def kernel(nrow, ncol, k_ref, v_ref, gram_ref, last_ref, *scratch):
     (
-        kv, kh, kl, vc, ktr, vg0, vg1, vtop, ps1, ps2, r1, s2, r2, zs, zr, mine,
+        kv, kk, vc, ktr, vg0, vg1, vtop, ps1, ps2, whole, r1, s2, r2, zs, zr, mine,
         ds1, dr1, ds2, dr2, hs, tp0, tg0, tg1, hp, hz,
         gs, gr, gp, gz, gq, ga,
         ld, kq, tps, z_sem, ag_sem, rs_sem, col_sem, top_sem, hz_sem, g_sem,
@@ -131,7 +156,18 @@
             body(k)
             return carry
 
-        lax.fori_loop(start, n, step, 0)
+        if n - start < 4:
+            for k in range(start, n):
+                body(k)
+        else:
+            lax.fori_loop(start, n, step, 0)
+
+    def farthest_first(n, body):
+        def step(k, carry):
+            body(lax.rem(n // 2 + lax.rem(k, 2) * (k + 1) // 2 + (1 - lax.rem(k, 2)) * (n - k // 2), n))
+            return carry
+
+        lax.fori_loop(0, n - 1, step, 0)
 
     def push(src, dst, s, r, where):
         pltpu.make_async_remote_copy(
@@ -164,6 +200,9 @@
         pl.when(b * ncol + col != row)(functools.partial(lambda b: greet(mirror(b)), b))
     pl.when(jnp.logical_not(self_held))(lambda: greet(holder()))
 
+    def to_plane(src, dst, s, r):
+        each(nxy, lambda k: push(src, dst, s, r, plane(k)))
+
     def held_one(p, act):
         same = jnp.logical_and(row * ncol + col == row, p == col)
         pl.when(jnp.logical_not(same))(act)
@@ -172,16 +211,6 @@
     def _():
         each(ncol, lambda p: held_one(p, lambda: greet(held_member(p))), 0)
 
-    for zd in range(2):
-        ps1[zd, 0, 0] = jnp.zeros((sub, tile), F32)
-        ps2[zd, 0, 0] = jnp.zeros((sub, tile), F32)
-    for n in range(loads):
-        load(n).wait()
-        for at in range(max(n * chunk, 2), (n + 1) * chunk):
-            q, zd = divmod(at, 2)
-            hi, lo = split(kv[at])
-            kh[zd, :, q * tile : (q + 1) * tile] = hi
-            kl[zd, :, q * tile : (q + 1) * tile] = lo
     load_v.wait()
 
     @pl.when(holds)
@@ -209,6 +238,9 @@
     low, high = pl.ds(0, sub // 2), pl.ds(sub // 2, sub // 2)
 
     def gather_start(src, vg, unit, zd):
+        if D_AG[unit]:
+            to_plane(src, vg.at[zd, y, x], s_ag.at[unit, 0, 0], ag_sem.at[unit, 0, 0])
+            return
         each(
             side,
             lambda k: push(
@@ -223,6 +255,8 @@
         )
 
     def gather_turn(vg, unit, zd):
+        if D_AG[unit]:
+            return
         take(vg.at[0, 0, pl.ds(0, side - 1), low], ag_sem.at[unit, 0, 0])
         part = vg.at[zd, y, :, low]
         each(side, lambda k: push(part, part, s_ag.at[unit, 0, 1], ag_sem.at[unit, 0, 1], along(0, k)))
@@ -231,6 +265,9 @@
         each(side, lambda k: push(rest, rest, s_ag.at[unit, 1, 1], ag_sem.at[unit, 1, 1], along(1, k)))
 
     def gather_end(vg, unit):
+        if D_AG[unit]:
+            take(whole.at[0, 0, pl.ds(0, nxy - 1)], ag_sem.at[unit, 0, 0])
+            return
         take(vg.at[0, pl.ds(0, side - 1), :, low], ag_sem.at[unit, 0, 1])
         take(vg.at[0, pl.ds(0, side - 1), :, low], ag_sem.at[unit, 1, 1])
 
@@ -239,22 +276,37 @@
 
         @pl.when(row < b * ncol + col)
         def _(b=b):
-            push(kv.at[b], ktr.at[home], s_one.at[4 + b], kq.at[home], mirror(b))
-
-    def to_plane(src, dst, s, r):
-        each(nxy, lambda k: push(src, dst, s, r, plane(k)))
+            push(k_ref.at[b], ktr.at[home], s_one.at[4 + b], kq.at[home], mirror(b))
 
     def upright(pieces):
         return pieces[...].reshape(tile, 2 * sub).T[:sub]
 
+    def paired(top):
+        hi, lo = split(top)
+        return jnp.concatenate(
+            [jnp.concatenate([hi, hi], axis=1), jnp.concatenate([lo, jnp.zeros_like(lo)], axis=1)], axis=0
+        )
+
     def spread_products(top, ps, it, turn):
-        hi, lo = top
         zd = other if turn == 0 else zh
-        wide = jnp.dot(jnp.concatenate([hi, lo], axis=0), kh[zd, :, tile:], preferred_element_type=F32)
+        wide = jnp.dot(top, kk[zd, :, tile:], preferred_element_type=F32)
         wide = wide[:sub] + wide[sub:]
-        wide = wide + jnp.dot(hi, kl[zd, :, tile:], preferred_element_type=F32)
         for q in range(1, nxy):
             ps[zd, q // side, q % side] = wide[:, (q - 1) * tile : q * tile]
+        if D_RS[it][turn]:
+
+            def whole_one(k):
+                at = lax.rem(xy + k, nxy)
+                push(
+                    ps.at[zd, at // side, lax.rem(at, side)],
+                    whole.at[it, turn, xy],
+                    s_rs.at[it, turn, 0, 0],
+                    rs_sem.at[it, turn, 0, 0],
+                    plane(k),
+                )
+
+            each(nxy, whole_one)
+            return
         for half, (axis, rows) in enumerate(((0, low), (1, high))):
 
             def one(k, half=half, axis=axis, rows=rows):
@@ -276,6 +328,8 @@
         return total
 
     def sum_turn(ps, it, turn):
+        if D_RS[it][turn]:
+            return
         zd = other if turn == 0 else zh
         for half, (axis, rows) in enumerate(((0, low), (1, high))):
             take(r1.at[0, 0, 0, pl.ds(0, side - 1)], rs_sem.at[it, turn, half, 0])
@@ -295,7 +349,14 @@
 
             each(side, one)
 
-    def sum_end(it, turn):
+    def sum_end(ps, it, turn):
+        if D_RS[it][turn]:
+            take(whole.at[0, 0, pl.ds(0, nxy - 1)], rs_sem.at[it, turn, 0, 0])
+            whole[it, turn, xy] = ps[other if turn == 0 else zh, y, x]
+            total = whole[it, turn, 0]
+            for n in range(1, nxy):
+                total = total + whole[it, turn, n]
+            return total
         halves = []
         for half in range(2):
             take(r2.at[0, 0, 0, pl.ds(0, side - 1)], rs_sem.at[it, turn, half, 1])
@@ -310,7 +371,8 @@
 
     def direct(zd, first, last):
         cols = slice(first * tile, last * tile)
-        return nt(kh[zd, :, cols], vc[zd, :, cols]) + nt(kl[zd, :, cols], vc[zd, :, cols])
+        both = nt(kk[zd, :, cols], vc[zd, :, cols])
+        return both[:tile] + both[tile:]
 
     def scatter_direct(total, ds, dr, n):
         total = total + pltpu.roll(total, sub, 1)
@@ -322,6 +384,10 @@
             push(ds.at[at], dr.at[col], s_col.at[n], col_sem.at[n], in_col(k))
 
         each(ncol, one)
+
+    def over_z(turn):
+        zs[turn] = sum_end(ps1, 0, turn)
+        push(zs.at[turn], zr.at[turn], s_one.at[1 + turn], z_sem.at[1 + turn], zpart)
 
     def line_sum(ref, count):
         total = ref[0]
@@ -351,7 +417,7 @@
         take(gr.at[it, pl.ds(0, nxy - 1)], g_sem.at[it, 0])
         gp[it] = line_sum(gr.at[it], nxy)
         gz[it, member] = gp[it]
-        each(
+        farthest_first(
             nline,
             lambda k: push(
                 gp.at[it], gz.at[it, member], s_g.at[it, 1], g_sem.at[it, 1], in_line(k)
@@ -367,142 +433,223 @@
     def gram_in(it):
         take(ga.at[it, pl.ds(0, nxy - 1)], g_sem.at[it, 2])
         packed = jnp.concatenate([ga[it, p] for p in range(nxy)], axis=0)
-        gram = jnp.concatenate([packed[:, :sub], packed[:, sub:]], axis=0)
-        return gram / order
-
-    gather_turn(vg0, 0, zh)
-
-    take(vg0.at[other, y, x], z_sem.at[0])
-    gather_start(vg0.at[other, y, x], vg0, 1, other)
-
-    @pl.when(self_held)
-    def _():
-        tp0[...] = hs[col]
-
-    @pl.when(jnp.logical_not(self_held))
-    def _():
-        take(tp0, tps.at[0])
-
-    tg0[col] = tp0[...]
-    each(ncol, lambda k: push(tp0, tg0.at[col], s_col.at[3], col_sem.at[3], in_col(k)))
-    gather_turn(vg0, 1, other)
-
-    for b in range(band):
-
-        @pl.when(row < b * ncol + col)
-        def _(b=b):
-            ktr[b] = kv[b]
-
-        @pl.when(row == b * ncol + col)
-        def _(b=b):
-            ktr[b] = 0.5 * (kv[b] + kv[b].T)
-
-        @pl.when(row > b * ncol + col)
-        def _(b=b):
-            take(ktr.at[b], kq.at[b])
-            ktr[b] = ktr[b].T
-
-        hi, lo = split(ktr[b])
-        kh[b, :, :tile] = hi
-        kl[b, :, :tile] = lo
-
-    gather_end(vg0, 0)
-    lay(vg0, zh, 0)
-    total = direct(zh, 0, nxy)
-
-    take(tg0.at[pl.ds(0, ncol - 1)], col_sem.at[3])
-    top = split(upright(tg0))
-    spread_products(top, ps1, 0, 0)
-
-    gather_end(vg0, 1)
-    lay(vg0, other, 0)
-    scatter_direct(total + direct(other, 0, nxy), ds1, dr1, 0)
-
-    spread_products(top, ps1, 0, 1)
-    sum_turn(ps1, 0, 0)
-
-    take(dr1.at[pl.ds(0, ncol - 1)], col_sem.at[0])
-    piece1 = line_sum(dr1, ncol)
-    tg1[col] = piece1
-    each(ncol, lambda k: push(tg1.at[col], tg1.at[col], s_col.at[1], col_sem.at[1], in_col(k)))
-
-    sum_turn(ps1, 0, 1)
-    for turn in range(2):
-        zs[turn] = sum_end(0, turn)
-        push(zs.at[turn], zr.at[turn], s_one.at[1 + turn], z_sem.at[1 + turn], zpart)
-
-    take(tg1.at[pl.ds(0, ncol - 1)], col_sem.at[1])
-    top = upright(tg1)
-
-    @pl.when(is_root)
-    def _():
-        mine[0] = top
-        push(mine.at[0], vtop.at[home], s_top.at[1], top_sem.at[home], zpart)
-        to_plane(mine.at[0], vtop.at[home], s_top.at[0], top_sem.at[home])
-        vtop[home] = top
-
-    parts = split(top)
-    spread_products(parts, ps2, 1, 0)
-
-    take(zr.at[0], z_sem.at[1])
-    mine[1] = zs[1] + zr[0]
-    vg1[zh, y, x] = mine[1]
-    gram_out(jnp.concatenate([mine[1], piece_tile(piece1)], axis=1), 0)
-    gather_start(mine.at[1], vg1, 2, zh)
-    spread_products(parts, ps2, 1, 1)
-    take(zr.at[1], z_sem.at[2])
-    mine[2] = zs[0] + zr[1]
-    vg1[other, y, x] = mine[2]
-    gather_start(mine.at[2], vg1, 3, other)
-
-    sum_turn(ps2, 1, 0)
-    gather_turn(vg1, 2, zh)
-    gram_line(0)
-    gather_turn(vg1, 3, other)
-    zs[2] = sum_end(1, 0)
-    push(zs.at[2], zr.at[2], s_one.at[3], z_sem.at[3], zpart)
+        return unpacked(packed) / order
+
+    kept = {}
+
+    def cut_kernel():
+        for zd in range(2):
+            ps1[zd, 0, 0] = jnp.zeros((sub, tile), F32)
+            ps2[zd, 0, 0] = jnp.zeros((sub, tile), F32)
+        for n in range(loads):
+            load(n).wait()
+            for at in range(max(n * chunk, 2), (n + 1) * chunk):
+                q, zd = divmod(at, 2)
+                hi, lo = split(kv[at])
+                kk[zd, :tile, q * tile : (q + 1) * tile] = hi
+                kk[zd, tile:, q * tile : (q + 1) * tile] = lo
+
+    def own_turn():
+        gather_turn(vg0, 0, zh)
+
+    def other_start():
+        take(vg0.at[other, y, x], z_sem.at[0])
+        gather_start(vg0.at[other, y, x], vg0, 1, other)
+
+    def other_turn():
+        gather_turn(vg0, 1, other)
+
+    def top_pieces():
+        @pl.when(self_held)
+        def _():
+            tp0[...] = hs[col]
+
+        @pl.when(jnp.logical_not(self_held))
+        def _():
+            take(tp0, tps.at[0])
+
+        tg0[col] = tp0[...]
+        each(ncol, lambda k: push(tp0, tg0.at[col], s_col.at[3], col_sem.at[3], in_col(k)))
+
+    def mirrored():
+        for b in range(band):
+
+            @pl.when(row < b * ncol + col)
+            def _(b=b):
+                ktr[b] = kv[b]
+
+            @pl.when(row == b * ncol + col)
+            def _(b=b):
+                ktr[b] = 0.5 * (kv[b] + kv[b].T)
+
+            @pl.when(row > b * ncol + col)
+            def _(b=b):
+                take(ktr.at[b], kq.at[b])
+                ktr[b] = ktr[b].T
+
+            hi, lo = split(ktr[b])
+            kk[b, :tile, :tile] = hi
+            kk[b, tile:, :tile] = lo
+
+    def direct_own():
+        gather_end(vg0, 0)
+        lay(vg0, zh, 0)
+        kept["direct"] = direct(zh, 0, nxy)
+
+    def direct_other():
+        gather_end(vg0, 1)
+        lay(vg0, other, 0)
+        scatter_direct(kept["direct"] + direct(other, 0, nxy), ds1, dr1, 0)
+
+    def spread_other():
+        take(tg0.at[pl.ds(0, ncol - 1)], col_sem.at[3])
+        kept["top"] = paired(upright(tg0))
+        spread_products(kept["top"], ps1, 0, 0)
+
+    def spread_own():
+        spread_products(kept["top"], ps1, 0, 1)
+
+    def turn_other():
+        sum_turn(ps1, 0, 0)
+
+    def turn_own():
+        sum_turn(ps1, 0, 1)
+
+    def z_other():
+        over_z(0)
+
+    def z_own():
+        over_z(1)
+
+    def direct_sum():
+        take(dr1.at[pl.ds(0, ncol - 1)], col_sem.at[0])
+        kept["piece"] = line_sum(dr1, ncol)
+        tg1[col] = kept["piece"]
+        each(ncol, lambda k: push(tg1.at[col], tg1.at[col], s_col.at[1], col_sem.at[1], in_col(k)))
+
+    def top_tile():
+        take(tg1.at[pl.ds(0, ncol - 1)], col_sem.at[1])
+        top = upright(tg1)
+        kept["top1"] = paired(top)
+
+        @pl.when(is_root)
+        def _():
+            mine[0] = top
+            push(mine.at[0], vtop.at[home], s_top.at[1], top_sem.at[home], zpart)
+            to_plane(mine.at[0], vtop.at[home], s_top.at[0], top_sem.at[home])
+            vtop[home] = top
+
+    def spread_other1():
+        spread_products(kept["top1"], ps2, 1, 0)
+
+    def spread_own1():
+        spread_products(kept["top1"], ps2, 1, 1)
+
+    def own_tile():
+        take(zr.at[0], z_sem.at[1])
+        mine[1] = zs[1] + zr[0]
+        vg1[zh, y, x] = mine[1]
+
+    def gram_start():
+        gram_out(jnp.concatenate([mine[1], piece_tile(kept["piece"])], axis=1), 0)
+
+    def own_start1():
+        gather_start(mine.at[1], vg1, 2, zh)
+
+    def other_start1():
+        take(zr.at[1], z_sem.at[2])
+        mine[2] = zs[0] + zr[1]
+        vg1[other, y, x] = mine[2]
+        gather_start(mine.at[2], vg1, 3, other)
+
+    def turn_other1():
+        sum_turn(ps2, 1, 0)
+
+    def turn_own1():
+        sum_turn(ps2, 1, 1)
+
+    def own_turn1():
+        gather_turn(vg1, 2, zh)
+
+    def other_turn1():
+        gather_turn(vg1, 3, other)
+
+    def gram_line0():
+        gram_line(0)
+
+    def gram_back0():
+        gram_back(0)
+
+    def z_other1():
+        zs[2] = sum_end(ps2, 1, 0)
+        push(zs.at[2], zr.at[2], s_one.at[3], z_sem.at[3], zpart)
 
     root_part = col == lax.rem(row + 1 - 2 * zh, ncol)
 
-    @pl.when(root_part)
-    def _():
-        take(vtop.at[home], top_sem.at[home])
-        to_plane(vtop.at[home], vtop.at[home], s_top.at[0], top_sem.at[home])
-
-    sum_turn(ps2, 1, 1)
-    gather_end(vg1, 2)
-    lay(vg1, zh, 1)
-    total = direct(zh, 1, nxy)
-    gather_end(vg1, 3)
-    lay(vg1, other, 1)
-    total = total + direct(other, 1, nxy)
-    gram_back(0)
-    for b in range(band):
-        own = jnp.logical_and(home == b, jnp.logical_or(is_root, root_part))
-        pl.when(jnp.logical_not(own))(functools.partial(lambda b: take(vtop.at[b], top_sem.at[b]), b))
-        hi, lo = split(vtop[b])
-        vc[b, :sub, :tile] = hi
-        vc[b, sub:, :tile] = lo
-        total = total + direct(b, 0, 1)
-    scatter_direct(total, ds2, dr2, 2)
-
-    rest = sum_end(1, 1)
-    first = factorize(gram_in(0))
-    back = first[:, sub:]
-
-    take(dr2.at[pl.ds(0, ncol - 1)], col_sem.at[2])
-    hp[...] = line_sum(dr2, ncol)
-
-    @pl.when(self_held)
-    def _():
-        hz[col] = hp[...]
-
-    @pl.when(jnp.logical_not(self_held))
-    def _():
-        push(hp, hz.at[col], s_h.at[1], hz_sem.at[0], holder())
-
+    def top_forward():
+        @pl.when(root_part)
+        def _():
+            take(vtop.at[home], top_sem.at[home])
+            to_plane(vtop.at[home], vtop.at[home], s_top.at[0], top_sem.at[home])
+
+    def direct_own1():
+        gather_end(vg1, 2)
+        lay(vg1, zh, 1)
+        kept["own1"] = direct(zh, 1, nxy)
+
+    def direct_other1():
+        gather_end(vg1, 3)
+        lay(vg1, other, 1)
+        kept["other1"] = direct(other, 1, nxy)
+
+    def direct_top1():
+        total = kept["own1"] + kept["other1"]
+        for b in range(band):
+            own = jnp.logical_and(home == b, jnp.logical_or(is_root, root_part))
+            pl.when(jnp.logical_not(own))(
+                functools.partial(lambda b: take(vtop.at[b], top_sem.at[b]), b)
+            )
+            hi, lo = split(vtop[b])
+            vc[b, :sub, :tile] = hi
+            vc[b, sub:, :tile] = lo
+            total = total + direct(b, 0, 1)
+        scatter_direct(total, ds2, dr2, 2)
+
+    def rest_own1():
+        kept["rest"] = sum_end(ps2, 1, 1)
+
+    def factor0():
+        kept["back"] = factorize(gram_in(0))[:, sub:]
+
+    def direct_sum1():
+        take(dr2.at[pl.ds(0, ncol - 1)], col_sem.at[2])
+        hp[...] = line_sum(dr2, ncol)
+
+        @pl.when(self_held)
+        def _():
+            hz[col] = hp[...]
+
+        @pl.when(jnp.logical_not(self_held))
+        def _():
+            push(hp, hz.at[col], s_h.at[1], hz_sem.at[0], holder())
+
+    steps = dict(
+        cut_kernel=cut_kernel, own_turn=own_turn, other_start=other_start, other_turn=other_turn,
+        top_pieces=top_pieces, mirrored=mirrored, direct_own=direct_own, direct_other=direct_other,
+        spread_other=spread_other, spread_own=spread_own, turn_other=turn_other, turn_own=turn_own,
+        z_other=z_other, z_own=z_own, direct_sum=direct_sum, top_tile=top_tile,
+        spread_other1=spread_other1, spread_own1=spread_own1, own_tile=own_tile, gram_start=gram_start,
+        own_start1=own_start1, other_start1=other_start1, turn_other1=turn_other1, turn_own1=turn_own1,
+        own_turn1=own_turn1, other_turn1=other_turn1, gram_line0=gram_line0, gram_back0=gram_back0,
+        z_other1=z_other1, top_forward=top_forward, direct_own1=direct_own1, direct_other1=direct_other1,
+        direct_top1=direct_top1, rest_own1=rest_own1, factor0=factor0, direct_sum1=direct_sum1,
+    )
+    for name in ORDER:
+        steps[name]()
+
+    back = kept["back"]
     take(zr.at[2], z_sem.at[3])
-    both = jnp.concatenate([rest + zr[2], piece_tile(hp[...])], axis=1)
+    both = jnp.concatenate([kept["rest"] + zr[2], piece_tile(hp[...])], axis=1)
     both = jnp.dot(back, both, precision=HI, preferred_element_type=F32)
     gram_out(both, 1)
     mine[3] = both[:, :tile]
@@ -515,13 +662,9 @@
         mine[3] = jnp.dot(back, upright(hz), precision=HI, preferred_element_type=F32)
 
     gram_back(1)
-    second = factorize(gram_in(1))
-    out_ref[...] = jnp.dot(second[:, sub:], mine[3], precision=HI, preferred_element_type=F32)
-    keep = lax.broadcasted_iota(jnp.int32, (sub, sub), 0) >= lax.broadcasted_iota(
-        jnp.int32, (sub, sub), 1
-    )
-    square = jnp.concatenate([second, second], axis=0).T[:sub, :sub]
-    chol_ref[...] = jnp.where(keep, square, 0.0)
+    take(ga.at[1, pl.ds(0, nxy - 1)], g_sem.at[1, 2])
+    gram_ref[...] = jnp.concatenate([ga[1, p] for p in range(nxy)], axis=0)
+    last_ref[...] = mine[3]
 
     many = nxy - 1
     take(mine.at[0], s_one.at[0])
@@ -532,6 +675,9 @@
             functools.partial(lambda b: take(kv.at[b], s_one.at[4 + b]), b)
         )
     for unit in range(4):
+        if D_AG[unit]:
+            take(whole.at[0, 0, pl.ds(0, many)], s_ag.at[unit, 0, 0])
+            continue
         for half in range(2):
             take(vg0.at[0, 0, pl.ds(0, side - 1), low], s_ag.at[unit, half, 0])
             take(vg0.at[0, pl.ds(0, side - 1), :, low], s_ag.at[unit, half, 1])
@@ -546,6 +692,9 @@
         take(tg1.at[pl.ds(0, ncol - 1)], s_col.at[n])
     for it in range(2):
         for turn in range(2):
+            if D_RS[it][turn]:
+                take(whole.at[0, 0, pl.ds(0, many)], s_rs.at[it, turn, 0, 0])
+                continue
             for half in range(2):
                 take(r1.at[0, 0, 0, pl.ds(0, side - 1)], s_rs.at[it, turn, half, 0])
                 take(r2.at[0, 0, 0, pl.ds(0, side - 1)], s_rs.at[it, turn, half, 1])
@@ -559,9 +708,7 @@
 
     @pl.when(jnp.logical_or(is_root, root_part))
     def _():
-        for n in range(side - 1):
-            take(vg0.at[0, n], s_top.at[0])
-        take(vg0.at[0, 0, pl.ds(0, side - 1)], s_top.at[0])
+        take(whole.at[0, 0, pl.ds(0, many)], s_top.at[0])
 
 
 def per_device(nrow, ncol, kernel_tiles, basis):
@@ -579,9 +726,10 @@
     planes = (2, side, nxy // side, sub, tile)
     scratch = [
         vmem((tiles, tile, tile)),
-        vmem((2, tile, nxy * tile), BF16), vmem((2, tile, nxy * tile), BF16),
+        vmem((2, 2 * tile, nxy * tile), BF16),
         vmem((2, 2 * sub, nxy * tile), BF16), vmem((band, tile, tile)),
         vmem(planes), vmem(planes), vmem((band, sub, tile)), vmem(planes), vmem(planes),
+        vmem((2, 2, nxy, sub, tile)),
         vmem(halves + (side,) + half), vmem(halves + half), vmem(halves + half),
         vmem((3, sub, tile)), vmem((3, sub, tile)), vmem((4, sub, tile)),
         vmem(pieces), vmem(pieces), vmem(pieces), vmem(pieces),
@@ -593,11 +741,11 @@
         dma(4 + band), dma(4, 2, 2), dma(2, 2, 2, 2), dma(4), dma(2), dma(2, 3), dma(2),
     ]
     flops = 2 * 3 * 4 * tiles * tile * tile * sub
-    out, chol = pl.pallas_call(
+    gram, last = pl.pallas_call(
         functools.partial(kernel, nrow, ncol),
         out_shape=(
+            jax.ShapeDtypeStruct((sub // 2, 2 * sub), F32),
             jax.ShapeDtypeStruct((sub, tile), F32),
-            jax.ShapeDtypeStruct((sub, sub), F32),
         ),
         in_specs=[pl.BlockSpec(memory_space=pltpu.HBM)] * 2,
         out_specs=(pl.BlockSpec(memory_space=pltpu.VMEM),) * 2,
@@ -610,6 +758,16 @@
         ),
         name="subspace",
     )(kernel_tiles[0, 0], basis.reshape(sub, tile))
+    out, chol = pl.pallas_call(
+        functools.partial(finish, nrow * ncol * tile),
+        out_shape=(
+            jax.ShapeDtypeStruct((sub, tile), F32),
+            jax.ShapeDtypeStruct((sub, sub), F32),
+        ),
+        in_specs=[pl.BlockSpec(memory_space=pltpu.VMEM)] * 2,
+        out_specs=(pl.BlockSpec(memory_space=pltpu.VMEM),) * 2,
+        name="finish",
+    )(gram, last)
     return out.reshape(sub, 1, 1, tile), chol
 
 

time: 113 us -> 110 us (0.973)
  local copies, waits for them, and re-layouts: 2.75 us -> 0 us
    pallas_call x1, Pallas kernels: 109 us -> 104 us  [per_device(): pl.pallas_call(functools.partial(kernel, nrow, ncol), out_shape=(jax.Shap...]
    pallas_call x0 -> x1, Pallas kernels: none -> 4.27 us  [per_device(): pl.pallas_call(functools.partial(finish, nrow * ncol * tile), out_shape=(...]
    unnamed x2 -> x0, local copies, waits for them, and re-layouts: 2.75 us -> none
where the time goes in v3:
time: 110 us; the launch traced here: 109 us
  Pallas kernels  109 us (99%)
    pallas_call x1, Pallas kernels, per_device(): pl.pallas_call(functools.partial(kernel, nrow, ncol), out_shape=(jax.Shap...  104 us
    pallas_call x1, Pallas kernels, per_device(): pl.pallas_call(functools.partial(finish, nrow * ncol * tile), out_shape=(...  4.27 us

profile of v3, /device:TPU:1, one launch (start us, length us, event | category | flops | bytes accessed | tf_op | source)
XLA Modules:
  0.0 109.3 jit_solution(15444765627737624802)
XLA Ops:
  0.6 104.4 %subspace.1 = (f32[32,128]{1,0:T(8,128)}, f32[64,128]{1,0:T(8,128)}) custom-call(f32[32,128,128]{2,1,0:T(8,128)} %bitcast.5, f32[64,128]{1,0:T(8,128)} %bitcast.6), custom_call_target="tpu_custom_call" | custom-call | flops 805306368 | bytes 2097152 | tf_op jit(solution)/shard_map/subspace/pallas_call | solution.py:744
  105.1 4.3 %finish.1 = (f32[64,128]{1,0:T(8,128)}, f32[64,64]{1,0:T(8,128)}) custom-call(f32[32,128]{1,0:T(8,128)} %get-tuple-element.6.gram_ref, f32[64,128]{1,0:T(8,128)} %get-tuple-element.7.last_ref), custom_call_target="tpu_custom_call" | custom-call | tf_op jit(solution)/shard_map/finish/pallas_call | solution.py:761

commit v4 on v3

--- a/solution.py
+++ b/solution.py
@@ -10,12 +10,12 @@
 MESH = pl.DeviceIdType.MESH
 ORDER = (
     "cut_kernel", "own_turn", "other_start", "top_pieces", "other_turn", "mirrored", "direct_own",
-    "spread_other", "direct_other", "spread_own", "turn_other", "direct_sum", "z_other", "turn_own", "z_own",
+    "direct_other", "spread_other", "spread_own", "turn_other", "direct_sum", "z_other", "turn_own", "z_own",
     "top_tile", "spread_other1", "own_tile", "gram_start", "own_start1", "spread_own1", "other_start1",
     "turn_other1", "own_turn1", "gram_line0", "other_turn1", "z_other1", "top_forward", "turn_own1",
     "gram_back0", "direct_own1", "direct_other1", "direct_top1", "rest_own1", "factor0", "direct_sum1",
 )
-D_AG = (False, True, False, False)
+D_AG = (True, True, False, False)
 D_RS = ((True, True), (False, False))
 HI = lax.Precision.HIGHEST
 F32 = jnp.float32

time: 110 us -> 110 us (level)
  no operation moved by 1% of the time
where the time goes in v4:
time: 110 us; the launch traced here: 109 us
  Pallas kernels  109 us (99%)
    pallas_call x1, Pallas kernels, per_device(): pl.pallas_call(functools.partial(kernel, nrow, ncol), out_shape=(jax.Shap...  105 us
    pallas_call x1, Pallas kernels, per_device(): pl.pallas_call(functools.partial(finish, nrow * ncol * tile), out_shape=(...  4.27 us

profile of v4, /device:TPU:1, one launch (start us, length us, event | category | flops | bytes accessed | tf_op | source)
XLA Modules:
  0.0 109.4 jit_solution(2885541526713648123)
XLA Ops:
  0.6 104.5 %subspace.1 = (f32[32,128]{1,0:T(8,128)}, f32[64,128]{1,0:T(8,128)}) custom-call(f32[32,128,128]{2,1,0:T(8,128)} %bitcast.5, f32[64,128]{1,0:T(8,128)} %bitcast.6), custom_call_target="tpu_custom_call" | custom-call | flops 805306368 | bytes 2097152 | tf_op jit(solution)/shard_map/subspace/pallas_call | solution.py:744
  105.2 4.3 %finish.1 = (f32[64,128]{1,0:T(8,128)}, f32[64,64]{1,0:T(8,128)}) custom-call(f32[32,128]{1,0:T(8,128)} %get-tuple-element.6.gram_ref, f32[64,128]{1,0:T(8,128)} %get-tuple-element.7.last_ref), custom_call_target="tpu_custom_call" | custom-call | tf_op jit(solution)/shard_map/finish/pallas_call | solution.py:761
